TPU v7x, 512 devices: a whole 4x8x8 slice. The times are simulated.
512 devices in a mesh: dp: 32 (over x_lo, y, core), mp: 16 (over x_hi, z).
Axes of the slice: x: 4 (x_hi: 2, x_lo: 2; x = x_hi * 2 + x_lo), y: 8, z: 8, core: 2. Of those that a mesh axis runs over, the one named last changes fastest.
Arguments:
- layer_input: bfloat16 [512, 2, 8192], P('dp', None, 'mp'), may hold values from -90 to 90
- input_norm_gain: bfloat16 [8192], P('mp'), may hold values from 0.25 to 1.75
- key_matrix: bfloat16 [8192, 1024], P('mp'), may hold values from -0.09375 to 0.09375
- value_matrix: bfloat16 [8192, 1024], P('mp'), may hold values from -0.09375 to 0.09375
- adapter_down_factors: bfloat16 [2048, 16, 8192], P('dp', None, 'mp'), may hold values from -0.0625 to 0.0625
- adapter_up_factors: bfloat16 [2048, 16, 1024], P('dp', None, 'mp'), may hold values from -0.75 to 0.75
- adapter_storage_spot: int32 [2048], replicated, may hold values from 0 to 2047, as said below
- flight_adapter_ids: int32 [64], replicated, may hold values from 0 to 2047, as said below
- row_adapter_slot: int32 [512, 1], P('dp'), may hold values from 0 to 63
- lengths: int32 [512], P('dp'), may hold values from 2 to 384, as said below
- queries: bfloat16 [512, 2, 16, 512], P('dp', None, 'mp'), may hold values from -5 to 5
- key_value_cache: bfloat16 [512, 16, 384, 128], P('dp', 'mp'), may hold values from -5 to 5
Outputs:
- context: bfloat16 [512, 2, 16, 512], P('dp', None, 'mp')
- newest_cache_entries: bfloat16 [512, 2, 16, 128], P('dp', None, 'mp')
Inputs may be any that keep to these rules, and one draw needn't show every extreme that they name: `adapter_storage_spot`: A permutation. Storage positions g * 64 to (g + 1) * 64 - 1 are those of adapter_down_factors and adapter_up_factors on index g of dp. Distinct ids. The storage positions adapter_storage_spot[flight_adapter_ids] fall at most 4 times into one block of 64 positions, and exactly 4 times into some block. `lengths`: some row has exactly 384.
All inputs are finite; a program needn't handle non-finite values.
Results may differ from a plain program's by a relative error of at most 0.0054.
Values may be sent and summed in bfloat16 or wider, within the bound.
A program may use at most 64 MiB of HBM per device.

v0:
```python
import math

import jax
import jax.numpy as jnp
from jax import lax
from jax.sharding import PartitionSpec as P

KEY_HEADS = 8
CAP = 4


NORM_EPSILON = 1e-05
ADAPTER_SCALE = 2.0
ROPE_LOG_BASE = math.log(500000.0)
MASKED_SCORE = -1e30


def partner(value, axis, bit):
    mask = 2**bit
    pairs = [(source, source ^ mask) for source in range(lax.axis_size(axis))]
    return lax.ppermute(value, axis, pairs)


def rotate_pieces(key_lin, lengths, half_head_index):
    half_head_width = key_lin.shape[3]
    decode_step_count = key_lin.shape[1]
    coords = (
        half_head_index[:, None] * half_head_width
        + jnp.arange(half_head_width, dtype=jnp.int32)[None, :]
    )
    pair_index = (coords // 2).astype(jnp.float32)
    frequency = jnp.exp(-(2.0 * pair_index / (2 * half_head_width)) * ROPE_LOG_BASE)
    position = (lengths[:, None] + jnp.arange(decode_step_count, dtype=jnp.int32)[None, :]).astype(
        jnp.float32
    )
    angles = position[:, :, None, None] * frequency[None, None, :, :]
    cosine = jnp.cos(angles[..., 0::2])
    sine_part = jnp.sin(angles[..., 0::2])
    even_part = key_lin[..., 0::2]
    odd_part = key_lin[..., 1::2]
    rotated = jnp.stack(
        [even_part * cosine - odd_part * sine_part, even_part * sine_part + odd_part * cosine],
        axis=-1,
    )
    return rotated.reshape(key_lin.shape)


def partial_scores(query_part, cache_part, fresh_part):
    over_cache = jnp.einsum(
        "rtpgd,rpcd->rtpgc", query_part, cache_part, preferred_element_type=jnp.float32
    )
    over_fresh = jnp.einsum(
        "rtpgd,rspd->rtpgs", query_part, fresh_part, preferred_element_type=jnp.float32
    )
    return jnp.concatenate([over_cache, over_fresh], axis=-1)


def shards(
    layer_input,
    input_norm_gain,
    key_matrix,
    value_matrix,
    adapter_down_factors,
    adapter_up_factors,
    adapter_storage_spot,
    flight_adapter_ids,
    row_adapter_slot,
    lengths,
    queries,
    key_value_cache,
):
    row_count, decode_step_count, width_local = layer_input.shape
    model_size = lax.axis_size("mp")
    hidden = layer_input.astype(jnp.float32)
    square_sums = lax.psum(jnp.sum(hidden * hidden, axis=-1), "mp")
    mean_square = square_sums[..., None] / (width_local * model_size)
    normalized_input = (
        hidden * lax.rsqrt(mean_square + NORM_EPSILON) * input_norm_gain.astype(jnp.float32)
    ).astype(jnp.bfloat16)
    query_group_count = adapter_down_factors.shape[0]
    down_factor_width = adapter_down_factors.shape[2]
    active_count = flight_adapter_ids.shape[0]
    slot_position = jnp.take(adapter_storage_spot, flight_adapter_ids)
    slot_owner = slot_position // query_group_count
    slot_local = slot_position % query_group_count
    slot_numbers = jnp.arange(active_count, dtype=jnp.int32)
    earlier = (slot_numbers[None, :] < slot_numbers[:, None]) & (
        slot_owner[None, :] == slot_owner[:, None]
    )
    slot_rank = jnp.sum(earlier.astype(jnp.int32), axis=1)
    my_group = lax.axis_index("dp")
    wanted = (slot_owner[None, :] == my_group) & (
        slot_rank[None, :] == jnp.arange(CAP, dtype=jnp.int32)[:, None]
    )
    selected_factors = jnp.sum(jnp.where(wanted, slot_local[None, :], 0), axis=1)
    locally_held = jnp.concatenate(
        [adapter_down_factors[selected_factors], adapter_up_factors[selected_factors]], axis=2
    )
    factors = lax.all_gather(locally_held, "dp", axis=0, tiled=True)
    slot_place = slot_owner * CAP + slot_rank
    row_place = slot_place[row_adapter_slot[:, 0]]
    row_factors = factors[row_place]
    down_factor_rows = row_factors[:, :, :down_factor_width]
    up_factor_rows = row_factors[:, :, down_factor_width:]
    flat = normalized_input.reshape(row_count * decode_step_count, width_local)
    key_part = jnp.dot(flat, key_matrix, preferred_element_type=jnp.float32).reshape(
        row_count, decode_step_count, -1
    )
    value_part = jnp.dot(flat, value_matrix, preferred_element_type=jnp.float32).reshape(
        row_count, decode_step_count, -1
    )
    rank_part = jnp.einsum(
        "nui,nsi->nus", normalized_input, down_factor_rows, preferred_element_type=jnp.float32
    )
    key_share, value_portion = (
        lax.psum_scatter(key_part, "mp", scatter_dimension=2, tiled=True),
        lax.psum_scatter(value_part, "mp", scatter_dimension=2, tiled=True),
    )
    rank_sum = lax.psum(rank_part, "mp")
    value_portion = value_portion + ADAPTER_SCALE * jnp.einsum(
        "jzb,jbv->jzv",
        rank_sum,
        up_factor_rows.astype(jnp.float32),
        precision=lax.Precision.HIGHEST,
    )
    piece_local = key_value_cache.shape[1]
    half_head_width = key_value_cache.shape[3] // 2
    portion_index = lax.axis_index("mp") * piece_local + jnp.arange(piece_local, dtype=jnp.int32)
    half_head_index = portion_index // KEY_HEADS
    key_rot = rotate_pieces(
        key_share.reshape(row_count, decode_step_count, piece_local, half_head_width),
        lengths,
        half_head_index,
    )
    new_key = key_rot.astype(jnp.bfloat16)
    new_value = value_portion.reshape(
        row_count, decode_step_count, piece_local, half_head_width
    ).astype(jnp.bfloat16)
    newest_cache_entries = jnp.concatenate([new_key, new_value], axis=-1)
    query_local = queries.reshape(row_count, decode_step_count, piece_local, -1, half_head_width)
    cache_keys = key_value_cache[..., :half_head_width]
    cache_values = key_value_cache[..., half_head_width:]
    swap_bit = model_size.bit_length() - 2
    own_scores = partial_scores(query_local, cache_keys, new_key)
    other_scores = partner(own_scores, "mp", swap_bit)
    scale = 1.0 / math.sqrt(2 * half_head_width)
    scores = (own_scores + other_scores) * scale
    slot_count = key_value_cache.shape[2]
    cache_valid = jnp.arange(slot_count, dtype=jnp.int32)[None, None, :] < lengths[:, None, None]
    cache_valid = jnp.broadcast_to(cache_valid, (row_count, decode_step_count, slot_count))
    causal = jnp.arange(decode_step_count)[None, :] <= jnp.arange(decode_step_count)[:, None]
    causal = jnp.broadcast_to(causal[None], (row_count, decode_step_count, decode_step_count))
    allowed = jnp.concatenate([cache_valid, causal], axis=-1)
    scores = jnp.where(allowed[:, :, None, None, :], scores, MASKED_SCORE)
    top_score = jnp.max(scores, axis=-1, keepdims=True)
    exp_scores = jnp.exp(scores - top_score)
    total = jnp.sum(exp_scores, axis=-1, keepdims=True)
    weights = (exp_scores / total).astype(jnp.bfloat16)
    context_part = jnp.einsum(
        "rtpgc,rpcd->rtpgd",
        weights[..., :slot_count],
        cache_values,
        preferred_element_type=jnp.float32,
    )
    context_part = context_part + jnp.einsum(
        "rtpgs,rspd->rtpgd",
        weights[..., slot_count:],
        new_value,
        preferred_element_type=jnp.float32,
    )
    context = context_part.astype(jnp.bfloat16).reshape(
        row_count, decode_step_count, piece_local, -1
    )
    return (context, newest_cache_entries)


def solution(mesh):
    return jax.shard_map(
        shards,
        mesh=mesh,
        in_specs=(
            P("dp", None, "mp"),
            P("mp"),
            P("mp", None),
            P("mp", None),
            P("dp", None, "mp"),
            P("dp", None, "mp"),
            P(),
            P(),
            P("dp", None),
            P("dp"),
            P("dp", None, "mp", None),
            P("dp", "mp", None, None),
        ),
        out_specs=(P("dp", None, "mp", None), P("dp", None, "mp", None)),
        check_vma=False,
    )
```

profile of v0, /device:TPU:16, one launch (start us, length us, event | category | flops | bytes accessed | tf_op | source)
XLA Modules:
  0.0 554.4 jit_solution(47549954708447528)
XLA Ops:
  8.0 0.0 copy-start
  8.0 0.0 reduce-scatter.7.cloned.1.call-start
  8.1 0.8 convert_element_type.66
  8.8 0.9 fusion.30
  9.7 0.1 copy.79
  9.8 48.1 %psum.14 = f32[16,2]{0,1:T(2,128)S(1)} all-reduce(f32[16,2]{0,1:T(2,128)S(1)} %copy.79), channel_id=1, replica_groups=mesh['dp'=32,'mp'=16] {'mp'}, use_global_device_ids=true, to_apply=%region_1.0 | all-reduce | flops 32 | bytes 256 | tf_op jit(solution)/shard_map/psum | solution.py:75
  57.9 0.1 copy.80
  58.0 0.9 fusion.32
  58.8 0.3 fusion.25
  59.1 0.5 copy.101
  59.7 1.4 reshape.350
  61.1 0.0 reduce-scatter.7.cloned.1.call-update
  61.1 0.0 reduce-scatter.9.cloned.1.call-start
  61.1 0.3 fusion.23
  61.4 0.0 copy-start.1
  61.4 0.5 copy.103
  62.0 0.0 copy-start.6
  62.0 0.0 copy-start.4
  62.0 0.0 copy-start.7
  62.0 1.4 reshape.352
  63.4 0.0 reduce-scatter.9.cloned.1.call-update
  63.4 0.0 all-gather.2.cloned.1.call-start
  63.5 0.8 gather_fusion
  64.3 0.2 convert_reduce_fusion
  64.5 0.1 select_reduce_fusion
  64.7 1.5 gather_fusion.2
  66.2 1.8 gather_fusion.1
  68.0 0.6 pad_maximum_fusion.1
  68.6 0.0 all-gather.2.cloned.1.call-update
  68.7 0.1 broadcast_multiply_fusion
  68.8 0.2 slice.30
  69.0 0.0 copy-done.4
  69.0 0.1 reshape.297
  69.1 0.7 gather_fusion.3
  69.8 0.6 fusion.6
  70.5 0.1 fusion.44
  70.6 188.4 %reduce-scatter.7.cloned.1.call-done = f32[64,32]{1,0:T(8,128)} async-done(((f32[1024,32]{1,0:T(8,128)}), f32[64,32]{1,0:T(8,128)}) %reduce-scatter.7.cloned.1.call-update) | async-done | bytes 8208
  258.9 0.9 reshape.351
  259.8 0.1 copy.102
  259.9 0.2 slice.31
  260.1 0.2 slice.29
  260.3 0.1 copy.82
  260.4 0.1 copy.94
  260.5 0.2 convolution_bitcast_fusion
  260.6 0.9 pad_maximum_fusion
  261.5 3.7 collective-permute-start
  265.3 0.1 iota_compare_fusion.1
  265.4 0.1 copy.90
  265.5 199.5 %reduce-scatter.9.cloned.1.call-done = f32[64,32]{1,0:T(8,128)} async-done(((f32[1024,32]{1,0:T(8,128)}), f32[64,32]{1,0:T(8,128)}) %reduce-scatter.9.cloned.1.call-update) | async-done | bytes 8208
  465.0 0.9 reshape.353
  465.9 0.1 copy.87
  465.9 0.0 collective-permute-done
  466.0 1.3 fusion.43
  467.2 0.2 fusion.27
  467.5 0.2 divide_convert_fusion
  467.7 0.0 all-gather.2.cloned.1.call-done
  467.7 2.3 gather_fusion.4
  470.0 0.2 fusion.28
  470.2 74.4 %psum.15 = f32[16,2,16]{2,1,0:T(2,128)S(1)} all-reduce(f32[16,2,16]{2,1,0:T(2,128)S(1)} %fusion.28), channel_id=1, replica_groups=mesh['dp'=32,'mp'=16] {'mp'}, use_global_device_ids=true, to_apply=%region_8.9 | all-reduce | flops 512 | bytes 4096 | tf_op jit(solution)/shard_map/psum | solution.py:119
  544.6 0.2 fusion.22
  544.8 0.1 fusion.33
  544.9 0.6 fusion.18
  545.5 0.7 reshape.302
  546.3 0.7 maximum_bitcast_fusion
  (29 shorter events, 0.2 us)
Async XLA Ops:
  8.0 50.8 %copy-start = (bf16[512,1024]{1,0:T(8,128)(2,1)S(1)}, bf16[512,1024]{1,0:T(8,128)(2,1)}, u32[]{:S(2)}) copy-start(bf16[512,1024]{1,0:T(8,128)(2,1)} %param.14) | copy-start | bytes 3145732
  8.0 250.9 %reduce-scatter.7.cloned.1.call-start = ((), (), s32[]{:S(2)}) async-start(), calls=%async_computation.3 | async-start | bytes 557056
  59.1 2.0 copy-start.3
  61.1 403.9 %reduce-scatter.9.cloned.1.call-start = ((), (), s32[]{:S(2)}) async-start(), calls=%async_computation.4 | async-start | bytes 557056
  61.4 2.1 copy-start.5
  61.4 2.1 copy-start.1
  62.0 6.7 %copy-start.6 = (s32[16]{0:T(128)S(1)}, s32[16]{0:T(128)}, u32[]{:S(2)}) copy-start(s32[16]{0:T(128)} %param.21) | copy-start | bytes 196
  62.0 7.0 %copy-start.4 = (bf16[16,2,1,512]{3,1,2,0:T(2,128)(2,1)S(1)}, bf16[16,2,1,512]{3,1,2,0:T(2,128)(2,1)}, u32[]{:S(2)}) copy-start(bf16[16,2,1,512]{3,1,2,0:T(2,128)(2,1)} %param.22) | copy-start | bytes 98308
  62.0 7.1 %copy-start.7 = (s32[16,1]{0,1:T(1,128)S(1)}, s32[16,1]{0,1:T(1,128)}, u32[]{:S(2)}) copy-start(s32[16,1]{0,1:T(1,128)} %param.20) | copy-start | bytes 196
  63.4 6.4 %copy-start.2 = (bf16[16,1,384,128]{3,2,1,0:T(8,128)(2,1)S(1)}, bf16[16,1,384,128]{3,2,1,0:T(8,128)(2,1)}, u32[]{:S(2)}) copy-start(bf16[16,1,384,128]{3,2,1,0:T(8,128)(2,1)} %param.23) | copy-start | bytes 4718596
  63.4 404.2 %all-gather.2.cloned.1.call-start = ((), (), s32[]{:S(2)}) async-start(), calls=%async_computation.2 | async-start | bytes 2703360 | tf_op jit(solution)/shard_map/all_gather | solution.py:99
  261.5 204.5 %collective-permute-start = (f32[16,2,1,8,386]{4,3,1,0,2:T(8,128)}, f32[16,2,1,8,386]{4,3,1,0,2:T(8,128)}, u32[]{:S(2)}, u32[]{:S(2)}) collective-permute-start(f32[16,2,1,8,386]{4,3,1,0,2:T(8,128)} %pad_maximum_fusion), channel_id=1, source_target_pairs={{0,8},{1,9},{2,10},{3,11},{4,12},{5,13},{6,14},{7,15},{8,0},{9,1},... | collective-permute-start | bytes 1185800 | tf_op jit(solution)/shard_map/ppermute | solution.py:21
Sparse Core Ops, SparseCore 0:
  61.2 197.6 reduce-scatter.6
  264.0 201.0 reduce-scatter.8
Sparse Core Ops, SparseCore 1:
  68.7 62.0 all-gather.1
where the time goes:
time: 555 us; the launch traced here: 554 us
  waiting for transfers between devices  388 us (70%)
  blocking collectives  122 us (22%)
  between operations  15.8 us (3%)
  local copies, waits for them, and re-layouts  14.8 us (3%)
  other arithmetic  6.98 us (1%)
    unnamed x5, waiting for transfers between devices  388 us
    psum x1, blocking collectives, shards(): rank_sum = lax.psum(rank_part, 'mp')  74.4 us
    psum x1, blocking collectives, shards(): square_sums = lax.psum(jnp.sum(hidden * hidden, axis=-1), 'mp')  48.1 us
  transfers between devices with their start and end apart: 4, of which 2 were waited for; matrix products, arithmetic and copies ran while one was open for 3% of the time, Pallas kernels for 0%

commit v1 on v0

v1 whole, which is shorter than its diff:
```python
import math

import jax
import jax.numpy as jnp
from jax import lax
from jax.experimental import pallas as pl
from jax.experimental.pallas import tpu as pltpu
from jax.sharding import PartitionSpec as P

MESH = pl.DeviceIdType.MESH
F32 = jnp.float32
BF16 = jnp.bfloat16

NORM_EPSILON = 1e-05
ROPE_LOG_BASE = math.log(500000.0)
MASKED_SCORE = -1e30

Y, Z = 8, 8
ROWS, STEPS, CAP, RANK = 16, 2, 4, 16
TOKENS = ROWS * STEPS
GROUPS, HALF, WIDTH, SLOTS = 8, 64, 512, 384
QROWS = TOKENS * GROUPS
BLOCK = CAP * RANK

ROW_OFFS = [(k, 0, 0) for k in (0, 4, 3, 5, 2, 6, 1, 7)]
FAC_OFFS = [(0, a, b) for a in range(2) for b in range(2)]
MP_OFFS = sorted(
    [(a, b) for a in range(2) for b in range(Z) if a or b], key=lambda o: -2 * o[0] - min(o[1], Z - o[1])
)
Z_OFFS = (4, 3, 5, 2, 6, 1, 7)
NR, NF = len(ROW_OFFS), len(FAC_OFFS)
MET = NR * TOKENS

NN = (((1,), (0,)), ((), ()))
NT = (((1,), (1,)), ((), ()))
TN = (((0,), (0,)), ((), ()))


def dot(a, b, dims):
    return lax.dot_general(a, b, dims, preferred_element_type=F32)


def iota(shape, axis):
    return lax.broadcasted_iota(jnp.int32, shape, axis)


def body(
    x_hbm, gain_hbm, k_hbm, v_hbm, down_hbm, up_hbm, spot_hbm, ids_hbm, slot_hbm, len_hbm, q_hbm, cache_hbm,
    ctx_ref, new_ref,
    x_v, gain_v, k_v, v_v, down_v, up_v, spot_v, ids_v, slot_v, len_v, q_v, cache_v,
    flat, qexp, qown, qfull, rows, tags, facs, zsend, zrecv, xsend, xrecv, qother,
    own, other, ctxs, mps, mprecv, rets, retrecv,
    load_sem, rows_s, rows_r, tags_s, tags_r, facs_s, facs_r, z_s, z_r, x_s, x_r, q_s, q_r, sc_s, sc_r,
    mp_s, mp_r, ret_s, ret_r,
):
    dp, mp = lax.axis_index("dp"), lax.axis_index("mp")
    x_lo, y, core = dp // (2 * Y), (dp // 2) % Y, dp % 2
    half, z = mp // Z, mp % Z

    def along_dp(off, sign):
        to_y = (y + (Y + sign * off[0])) % Y
        return (((x_lo + off[1]) % 2) * (2 * Y) + to_y * 2 + (core + off[2]) % 2, mp)

    def along_mp(off):
        return (dp, ((half + off[0]) % 2) * Z + (z + off[1]) % Z)

    partner = (dp, (1 - half) * Z + z)

    barrier = pltpu.get_barrier_semaphore()
    greeted = [along_dp(o, 1) for o in ROW_OFFS + FAC_OFFS if o != (0, 0, 0)]
    greeted += [along_mp(o) for o in MP_OFFS]
    for device in greeted:
        pl.semaphore_signal(barrier, inc=1, device_id=device, device_id_type=MESH)

    def load(src, dst, n):
        copy = pltpu.make_async_copy(src, dst, load_sem.at[n])
        copy.start()
        return copy

    small = [
        load(x_hbm, x_v, 0), load(gain_hbm, gain_v, 1), load(spot_hbm, spot_v, 2), load(ids_hbm, ids_v, 3),
        load(slot_hbm, slot_v, 4), load(len_hbm, len_v, 5), load(q_hbm, q_v, 6),
    ]
    load_down, load_up = load(down_hbm, down_v, 7), load(up_hbm, up_v, 8)
    load_k, load_v = load(k_hbm, k_v, 9), load(v_hbm, v_v, 10)
    load_cache = load(cache_hbm, cache_v, 11)

    def send(src, dst, ss, rs, device):
        copy = pltpu.make_async_remote_copy(
            src_ref=src, dst_ref=dst, send_sem=ss, recv_sem=rs, device_id=device, device_id_type=MESH
        )
        copy.start()
        return copy

    for copy in small:
        copy.wait()

    for r in range(ROWS):
        flat[pl.ds(2 * r, 2), :] = x_v[r].astype(F32)
    hidden = flat[...]
    gained = (hidden * gain_v[...].astype(F32).reshape(1, WIDTH)).astype(BF16)
    rows[0] = gained
    square = jnp.sum(hidden * hidden, axis=1, keepdims=True)
    lane_t, sub_t = iota((TOKENS, 128), 1), iota((TOKENS, 128), 0)
    diagonal = lane_t == sub_t
    square_row = jnp.sum(jnp.where(diagonal, square, 0.0), axis=0, keepdims=True)

    sub16, lane16 = iota((ROWS, 128), 0), iota((ROWS, 128), 1)
    slot_wide = jnp.pad(slot_v[...].astype(F32), ((0, 0), (0, 128 - ROWS)))
    slot_col = jnp.sum(jnp.where(sub16 == lane16, slot_wide, 0.0), axis=1, keepdims=True)
    tag_row = jnp.sum(
        jnp.where(sub16 == (lane16 % TOKENS) // STEPS, slot_col, 0.0), axis=0, keepdims=True
    )
    tags[0] = jnp.broadcast_to(tag_row, (8, 128))

    sub64, lane64 = iota((64, 64), 0), iota((64, 64), 1)
    ids_col = jnp.sum(jnp.where(sub64 == lane64, ids_v[...].astype(F32), 0.0), axis=1, keepdims=True)
    spots = spot_v[...].astype(F32)
    lane_n = iota((64, 128), 1).astype(F32)
    found = jnp.zeros((64, 128), F32)
    for i in range(16):
        found = found + jnp.where(ids_col - (128.0 * i) == lane_n, spots[i : i + 1, :], 0.0)
    place_col = jnp.sum(found, axis=1, keepdims=True)
    place_row = jnp.sum(jnp.where(sub64 == lane64, place_col, 0.0), axis=0, keepdims=True)
    group = dp.astype(F32)
    owner_row = jnp.floor(place_row * (1.0 / 64))
    mine_row = jnp.where(owner_row == group, 1.0, 0.0)
    mine_col = jnp.where(jnp.floor(place_col * (1.0 / 64)) == group, 1.0, 0.0)
    order_row = jnp.sum(jnp.where(sub64 < lane64, mine_col, 0.0), axis=0, keepdims=True)
    sub_f = (sub64 // RANK).astype(F32)
    picks = jnp.where(order_row == sub_f, mine_row, 0.0)
    target = jnp.sum(picks * (place_row - 64.0 * owner_row), axis=1, keepdims=True) * RANK
    target = target + (iota((64, 1), 0) % RANK).astype(F32)
    tag_col = jnp.sum(picks * (lane64 + 1).astype(F32), axis=1, keepdims=True) - 1.0
    select = jnp.where(target == iota((64, 1024), 1).astype(F32), 1.0, 0.0).astype(BF16)

    load_down.wait()
    facs[0, :, 0:WIDTH] = dot(select, down_v[...].reshape(64 * RANK, WIDTH), NN).astype(BF16)
    load_up.wait()
    up_own = dot(select, up_v[...].reshape(64 * RANK, HALF), NN).astype(BF16)
    shift = jnp.where(iota((HALF, 128), 1) == iota((HALF, 128), 0) + HALF, 1.0, 0.0).astype(BF16)
    up_wide = dot(up_own, shift, NN)
    facs[0, :, WIDTH : WIDTH + 128] = jnp.where(iota((64, 128), 1) < HALF, tag_col, up_wide).astype(BF16)

    pl.semaphore_wait(barrier, len(greeted))

    row_copies, tag_copies, fac_copies = [], [], []
    for k in range(1, NR):
        to = along_dp(ROW_OFFS[k], 1)
        row_copies.append(send(rows.at[0], rows.at[k], rows_s.at[k], rows_r.at[k], to))
        tag_copies.append(send(tags.at[0], tags.at[k], tags_s.at[k], tags_r.at[k], to))
    for k in range(1, NF):
        to = along_dp(FAC_OFFS[k], 1)
        fac_copies.append(send(facs.at[0], facs.at[k], facs_s.at[k], facs_r.at[k], to))
    q_copy = send(q_v, qother, q_s.at[0], q_r.at[0], partner)

    low = lane_t < HALF
    square_rows = jnp.broadcast_to(square_row, (8, 128))
    for w, (copy, weight) in enumerate(((load_k, k_v), (load_v, v_v))):
        copy.wait()
        part = dot(gained, weight[...], NN)
        here = slice(w * 128, w * 128 + 128)
        for j in range(4):
            first = part[:, j * 128 : j * 128 + 128]
            second = part[:, 512 + j * 128 : 512 + j * 128 + 128]
            zsend[2 * j, 0:TOKENS, here] = jnp.where(low, first, pltpu.roll(second, HALF, 1))
            zsend[2 * j + 1, 0:TOKENS, here] = jnp.where(low, pltpu.roll(first, HALF, 1), second)
        for j in range(Z):
            zsend[j, TOKENS : TOKENS + 8, here] = square_rows
    z_copies = [
        send(zsend.at[(z + k) % Z], zrecv.at[k], z_s.at[k], z_r.at[k], along_mp((0, k))) for k in Z_OFFS
    ]

    def expand(ref):
        for r in range(ROWS):
            flat[pl.ds(2 * r, 2), :] = ref[r].astype(F32)
        for g in range(GROUPS):
            tile = flat[:, (g // 2) * 128 : (g // 2) * 128 + 128]
            if g % 2:
                tile = pltpu.roll(tile, HALF, 1)
            qexp[pl.ds(g, TOKENS, stride=GROUPS), :] = jnp.where(low, tile, 0.0)
        return qexp[...]

    own_query = expand(q_v)
    qown[...] = own_query.astype(BF16)
    load_cache.wait()
    score_copies = []
    for c in range(4):
        for r in range(4 * c, 4 * c + 4):
            here = pl.ds(16 * r, 16)
            own[here, :] = dot(qown[here, :], cache_v[r], NT)
        here = pl.ds(64 * c, 64)
        score_copies.append(send(own.at[here], other.at[here], sc_s.at[c], sc_r.at[c], partner))

    for copy in row_copies + tag_copies + fac_copies:
        copy.wait_recv()
    lane_r = iota((8, 128), 1)
    tag_tiles = []
    for j in range((NR + 3) // 4):
        tile = jnp.zeros((8, 128), F32)
        for k in range(4 * j, min(4 * j + 4, NR)):
            tile = jnp.where(lane_r // TOKENS == k % 4, tags[k], tile)
        tag_tiles.append(tile)
    tag_all = jnp.concatenate(tag_tiles, axis=1)[0:1, :MET]
    fac_tag = facs[:, :, WIDTH : WIDTH + 128].reshape(NF * BLOCK, 128)[:, 0:1].astype(F32)
    same = fac_tag == tag_all
    met = dot(
        facs[:, :, 0:WIDTH].reshape(NF * BLOCK, WIDTH), rows[...].reshape(MET, WIDTH), NT
    )
    rank_part = jnp.sum(jnp.where(same, met, 0.0).reshape(NF * CAP, RANK, MET), axis=0)
    mps[...] = rank_part.astype(BF16)
    mp_copies = [
        send(mps, mprecv.at[k], mp_s.at[k], mp_r.at[k], along_mp(o)) for k, o in enumerate(MP_OFFS)
    ]

    for copy in z_copies:
        copy.wait_recv()
    total = zsend[z]
    for k in range(1, Z):
        total = total + zrecv[k]
    xsend[...] = total
    x_copy = send(xsend, xrecv, x_s.at[0], x_r.at[0], partner)

    q_copy.wait_recv()
    other_query = expand(qother)
    upper = half == 1
    first = jnp.where(upper, other_query, own_query)
    second = jnp.where(upper, own_query, other_query)
    qfull[...] = (first + pltpu.roll(second, HALF, 1)).astype(BF16)

    scale = 1.0 / math.sqrt(2 * HALF)
    len_wide = jnp.pad(len_v[...].astype(F32), ((0, 0), (0, 128 - ROWS)))
    len_col = jnp.sum(
        jnp.where(iota((QROWS, 128), 1) == iota((QROWS, 128), 0) // 16, len_wide, 0.0), axis=1, keepdims=True
    )
    cache_tops, cache_sums = [], []
    for c in range(4):
        score_copies[c].wait_recv()
        here = pl.ds(64 * c, 64)
        scores = (own[here, :] + other[here, :]) * scale
        valid = iota((64, SLOTS), 1).astype(F32) < len_col[64 * c : 64 * c + 64]
        scores = jnp.where(valid, scores, MASKED_SCORE)
        top = jnp.max(scores, axis=1, keepdims=True)
        spread = jnp.exp(scores - top)
        cache_tops.append(top)
        cache_sums.append(jnp.sum(spread, axis=1, keepdims=True))
        spread = spread.astype(BF16)
        for r in range(4):
            ctxs[pl.ds(64 * c + 16 * r, 16), :] = dot(spread[16 * r : 16 * r + 16], cache_v[4 * c + r], NN)
    cache_top = jnp.concatenate(cache_tops, axis=0)
    cache_sum = jnp.concatenate(cache_sums, axis=0)

    x_copy.wait_recv()
    total = xsend[...] + xrecv[...]
    squares = jnp.sum(jnp.where(diagonal, total[TOKENS : TOKENS + 1, 0:128], 0.0), axis=1, keepdims=True)
    norm = lax.rsqrt(squares * (1.0 / (16 * WIDTH)) + NORM_EPSILON)
    key_lin = total[0:TOKENS, 0:128] * norm
    pair = (lane_t // 2).astype(F32)
    frequency = jnp.exp(-(2.0 * pair / (2 * HALF)) * ROPE_LOG_BASE)
    start = jnp.sum(jnp.where(lane_t == sub_t // STEPS, len_wide, 0.0), axis=1, keepdims=True)
    angle = (start + (sub_t % STEPS).astype(F32)) * frequency
    even = lane_t % 2 == 0
    turned = jnp.where(even, -pltpu.roll(key_lin, 127, 1), pltpu.roll(key_lin, 1, 1))
    key_rot = key_lin * jnp.cos(angle) + turned * jnp.sin(angle)
    new_key = key_rot.astype(BF16)
    fresh = dot(qfull[...], new_key, NT) * scale
    q_sub, t_lane = iota((QROWS, TOKENS), 0), iota((QROWS, TOKENS), 1)
    counts = (t_lane // STEPS == q_sub // 16) & (t_lane % STEPS <= (q_sub // GROUPS) % STEPS)
    fresh = jnp.where(counts, fresh, MASKED_SCORE)
    top = jnp.maximum(cache_top, jnp.max(fresh, axis=1, keepdims=True))
    fresh_exp = jnp.exp(fresh - top)
    shrink = jnp.exp(cache_top - top)
    inverse = 1.0 / (cache_sum * shrink + jnp.sum(fresh_exp, axis=1, keepdims=True))
    fresh_weights = (fresh_exp * inverse).astype(BF16)
    ctxs[...] = ctxs[...] * (shrink * inverse)
    key_own = jnp.where(upper, pltpu.roll(key_rot, HALF, 1), key_rot)
    value_base = total[0:TOKENS, 128:256]
    value_base = jnp.where(upper, value_base, pltpu.roll(value_base, HALF, 1))

    for copy in mp_copies:
        copy.wait_recv()
    rank = rank_part
    for k in range(15):
        rank = rank + mprecv[k].astype(F32)
    spread = jnp.broadcast_to(rank[None], (NF * CAP, RANK, MET)).reshape(NF * BLOCK, MET)
    spread = jnp.where(same, spread, 0.0)
    up_all = facs[:, :, WIDTH : WIDTH + 128].reshape(NF * BLOCK, 128)
    coarse = spread.astype(BF16)
    rest = (spread - coarse.astype(F32)).astype(BF16)
    rets[...] = (dot(coarse, up_all, TN) + dot(rest, up_all, TN)).reshape(NR, TOKENS, 128)
    ret_copies = [
        send(rets.at[k], retrecv.at[k], ret_s.at[k], ret_r.at[k], along_dp(ROW_OFFS[k], -1))
        for k in range(1, NR)
    ]
    lora = rets[0]
    for copy in ret_copies:
        copy.wait_recv()
    for k in range(1, NR):
        lora = lora + retrecv[k]

    new_value = ((value_base + 2.0 * lora) * norm).astype(BF16)
    new_ref[...] = jnp.where(low, key_own, ((value_base + 2.0 * lora) * norm)).astype(BF16)
    qexp[...] = ctxs[...] + dot(fresh_weights, new_value, NN)
    for j in range(4):
        left = qexp[pl.ds(2 * j, TOKENS, stride=GROUPS), :]
        right = qexp[pl.ds(2 * j + 1, TOKENS, stride=GROUPS), :]
        ctx_ref[:, j * 128 : j * 128 + 128] = jnp.where(low, pltpu.roll(left, HALF, 1), right).astype(BF16)

    for copy in (
        row_copies + tag_copies + fac_copies + z_copies + score_copies + mp_copies + ret_copies + [q_copy, x_copy]
    ):
        copy.wait_send()


def shards(
    layer_input, input_norm_gain, key_matrix, value_matrix, adapter_down_factors, adapter_up_factors,
    adapter_storage_spot, flight_adapter_ids, row_adapter_slot, lengths, queries, key_value_cache,
):
    dma = pltpu.SemaphoreType.DMA
    loads = [
        ((ROWS, STEPS, WIDTH), BF16), ((WIDTH,), BF16), ((WIDTH, 1024), BF16), ((WIDTH, 1024), BF16),
        ((64, RANK, WIDTH), BF16), ((64, RANK, HALF), BF16), ((16, 128), jnp.int32), ((1, 64), jnp.int32),
        ((1, ROWS), jnp.int32), ((1, ROWS), jnp.int32), ((ROWS, STEPS, WIDTH), BF16), ((ROWS, SLOTS, 128), BF16),
    ]
    work = [
        ((TOKENS, WIDTH), F32),
        ((QROWS, 128), F32),
        ((QROWS, 128), BF16),
        ((QROWS, 128), BF16),
        ((NR, TOKENS, WIDTH), BF16),
        ((NR, 8, 128), F32),
        ((NF, BLOCK, WIDTH + 128), BF16),
        ((Z, TOKENS + 8, 256), F32),
        ((Z, TOKENS + 8, 256), F32),
        ((TOKENS + 8, 256), F32),
        ((TOKENS + 8, 256), F32),
        ((ROWS, STEPS, WIDTH), BF16),
        ((QROWS, SLOTS), F32),
        ((QROWS, SLOTS), F32),
        ((QROWS, 128), F32),
        ((RANK, MET), BF16),
        ((15, RANK, MET), BF16),
        ((NR, TOKENS, 128), F32),
        ((NR, TOKENS, 128), F32),
    ]
    sems = [12, NR, NR, NR, NR, NF, NF, Z, Z, 1, 1, 1, 1, 4, 4, 15, 15, NR, NR]
    any_spec = pl.BlockSpec(memory_space=pl.ANY)
    vmem_spec = pl.BlockSpec(memory_space=pltpu.VMEM)
    context, newest = pl.pallas_call(
        body,
        out_shape=(
            jax.ShapeDtypeStruct((TOKENS, WIDTH), BF16),
            jax.ShapeDtypeStruct((TOKENS, 128), BF16),
        ),
        in_specs=[any_spec] * 12,
        out_specs=(vmem_spec, vmem_spec),
        scratch_shapes=[pltpu.VMEM(*s) for s in loads + work] + [dma((n,)) for n in sems],
        compiler_params=pltpu.CompilerParams(
            collective_id=0, has_side_effects=True, vmem_limit_bytes=40 * 2**20
        ),
    )(*(pltpu.with_memory_space_constraint(a, pltpu.HBM) for a in (
        layer_input,
        input_norm_gain,
        key_matrix,
        value_matrix,
        adapter_down_factors,
        adapter_up_factors,
        adapter_storage_spot.reshape(16, 128),
        flight_adapter_ids.reshape(1, 64),
        row_adapter_slot.reshape(1, ROWS),
        lengths.reshape(1, ROWS),
        queries.reshape(ROWS, STEPS, WIDTH),
        key_value_cache.reshape(ROWS, SLOTS, 128),
    )))
    return context.reshape(ROWS, STEPS, 1, WIDTH), newest.reshape(ROWS, STEPS, 1, 128)


def solution(mesh):
    return jax.shard_map(
        shards,
        mesh=mesh,
        in_specs=(
            P("dp", None, "mp"),
            P("mp"),
            P("mp", None),
            P("mp", None),
            P("dp", None, "mp"),
            P("dp", None, "mp"),
            P(),
            P(),
            P("dp", None),
            P("dp"),
            P("dp", None, "mp", None),
            P("dp", "mp", None, None),
        ),
        out_specs=(P("dp", None, "mp", None), P("dp", None, "mp", None)),
        check_vma=False,
    )
```

time: 555 us -> 40.7 us (0.07)
  the two profiles are of different devices: /device:TPU:16 before, /device:TPU:4 now
where the time goes in v1:
time: 40.7 us; the launch traced here: 40.6 us
  Pallas kernels  38.7 us (95%)
  local copies, waits for them, and re-layouts  1.23 us (3%)
  between operations  0.64 us (2%)
    pallas_call x1, Pallas kernels, shards(): pl.pallas_call(body, out_shape=(jax.ShapeDtypeStruct((TOKENS, WIDTH), BF1...  38.7 us

profile of v1, /device:TPU:4, one launch (start us, length us, event | category | flops | bytes accessed | tf_op | source)
XLA Modules:
  0.0 40.6 jit_solution(13018027284024051157)
XLA Ops:
  0.6 38.7 %shard_map.131 = (bf16[32,512]{1,0:T(8,128)(2,1)S(1)}, bf16[32,128]{1,0:T(8,128)(2,1)S(1)}) custom-call(bf16[16,2,512]{2,1,0:T(2,128)(2,1)} %x_hbm.1, bf16[512]{0:T(512)(128)(2,1)} %gain_hbm.1, bf16[512,1024]{1,0:T(8,128)(2,1)} %k_hbm.1, bf16[512,1024]{1,0:T(8,128)(2,1)} %v_hbm.1, bf16[64,16,512]{2,1,0:T(8,128)(2,1)} %down_hbm.1, ...), custom_call_target="tpu_custom_call" | custom-call | tf_op jit(solution)/shard_map/pallas_call | solution.py:349
  39.4 0.6 %reshape.34 = bf16[16,2,1,512]{3,1,0,2:T(2,128)(2,1)} reshape(bf16[32,512]{1,0:T(8,128)(2,1)S(1)} %get-tuple-element.4) | data formatting | bytes 65536 | tf_op jit(solution)/shard_map/reshape | solution.py:375
  40.0 0.6 %copy.17 = bf16[16,2,1,128]{3,1,2,0:T(2,128)(2,1)} copy(bf16[16,2,1,128]{3,1,2,0:T(2,128)(2,1)S(1)} %bitcast.10) | data formatting | bytes 16384

commit v2 on v1

--- a/solution.py
+++ b/solution.py
@@ -44,13 +44,27 @@
     return lax.broadcasted_iota(jnp.int32, shape, axis)
 
 
+CODE_RATE, CODE_SHIFT = 1.75, 124.0
+
+
+def encode(score):
+    power = jnp.exp2(jnp.abs(score) * CODE_RATE - CODE_SHIFT)
+    return jnp.where(score < 0.0, -power, power).astype(BF16)
+
+
+def decode(code):
+    power = code.astype(F32)
+    size = (jnp.log2(jnp.abs(power)) + CODE_SHIFT) * (1.0 / CODE_RATE)
+    return jnp.where(power < 0.0, -size, size)
+
+
 def body(
     x_hbm, gain_hbm, k_hbm, v_hbm, down_hbm, up_hbm, spot_hbm, ids_hbm, slot_hbm, len_hbm, q_hbm, cache_hbm,
     ctx_ref, new_ref,
     x_v, gain_v, k_v, v_v, down_v, up_v, spot_v, ids_v, slot_v, len_v, q_v, cache_v,
-    flat, qexp, qown, qfull, rows, tags, facs, zsend, zrecv, xsend, xrecv, qother,
-    own, other, ctxs, mps, mprecv, rets, retrecv,
-    load_sem, rows_s, rows_r, tags_s, tags_r, facs_s, facs_r, z_s, z_r, x_s, x_r, q_s, q_r, sc_s, sc_r,
+    flat, qexp, qown, qfull, rows, facs, zsend, zrecv, xsend, xrecv, qother,
+    own, coded, other, ctxs, mps, mprecv, rets, retrecv,
+    load_sem, rows_s, rows_r, facs_s, facs_r, z_s, z_r, x_s, x_r, q_s, q_r, sc_s, sc_r,
     mp_s, mp_r, ret_s, ret_r,
 ):
     dp, mp = lax.axis_index("dp"), lax.axis_index("mp")
@@ -99,7 +113,8 @@
         flat[pl.ds(2 * r, 2), :] = x_v[r].astype(F32)
     hidden = flat[...]
     gained = (hidden * gain_v[...].astype(F32).reshape(1, WIDTH)).astype(BF16)
-    rows[0] = gained
+    for j in range(4):
+        rows[0, TOKENS * j : TOKENS * j + TOKENS, :] = gained[:, 128 * j : 128 * j + 128]
     square = jnp.sum(hidden * hidden, axis=1, keepdims=True)
     lane_t, sub_t = iota((TOKENS, 128), 1), iota((TOKENS, 128), 0)
     diagonal = lane_t == sub_t
@@ -111,8 +126,13 @@
     tag_row = jnp.sum(
         jnp.where(sub16 == (lane16 % TOKENS) // STEPS, slot_col, 0.0), axis=0, keepdims=True
     )
-    tags[0] = jnp.broadcast_to(tag_row, (8, 128))
-
+    rows[0, 4 * TOKENS : 4 * TOKENS + 16, :] = jnp.broadcast_to(tag_row, (16, 128)).astype(BF16)
+
+    pl.semaphore_wait(barrier, len(greeted))
+
+    row_copies = [
+        send(rows.at[0], rows.at[k], rows_s.at[k], rows_r.at[k], along_dp(ROW_OFFS[k], 1)) for k in range(1, NR)
+    ]
     sub64, lane64 = iota((64, 64), 0), iota((64, 64), 1)
     ids_col = jnp.sum(jnp.where(sub64 == lane64, ids_v[...].astype(F32), 0.0), axis=1, keepdims=True)
     spots = spot_v[...].astype(F32)
@@ -142,16 +162,9 @@
     up_wide = dot(up_own, shift, NN)
     facs[0, :, WIDTH : WIDTH + 128] = jnp.where(iota((64, 128), 1) < HALF, tag_col, up_wide).astype(BF16)
 
-    pl.semaphore_wait(barrier, len(greeted))
-
-    row_copies, tag_copies, fac_copies = [], [], []
-    for k in range(1, NR):
-        to = along_dp(ROW_OFFS[k], 1)
-        row_copies.append(send(rows.at[0], rows.at[k], rows_s.at[k], rows_r.at[k], to))
-        tag_copies.append(send(tags.at[0], tags.at[k], tags_s.at[k], tags_r.at[k], to))
-    for k in range(1, NF):
-        to = along_dp(FAC_OFFS[k], 1)
-        fac_copies.append(send(facs.at[0], facs.at[k], facs_s.at[k], facs_r.at[k], to))
+    fac_copies = [
+        send(facs.at[0], facs.at[k], facs_s.at[k], facs_r.at[k], along_dp(FAC_OFFS[k], 1)) for k in range(1, NF)
+    ]
     q_copy = send(q_v, qother, q_s.at[0], q_r.at[0], partner)
 
     low = lane_t < HALF
@@ -181,37 +194,42 @@
             qexp[pl.ds(g, TOKENS, stride=GROUPS), :] = jnp.where(low, tile, 0.0)
         return qexp[...]
 
+    scale = 1.0 / math.sqrt(2 * HALF)
     own_query = expand(q_v)
     qown[...] = own_query.astype(BF16)
     load_cache.wait()
-    score_copies = []
-    for c in range(4):
-        for r in range(4 * c, 4 * c + 4):
-            here = pl.ds(16 * r, 16)
-            own[here, :] = dot(qown[here, :], cache_v[r], NT)
-        here = pl.ds(64 * c, 64)
-        score_copies.append(send(own.at[here], other.at[here], sc_s.at[c], sc_r.at[c], partner))
-
-    for copy in row_copies + tag_copies + fac_copies:
+    for r in range(ROWS):
+        here = pl.ds(16 * r, 16)
+        piece = dot(qown[here, :], cache_v[r], NT) * scale
+        own[here, :] = piece
+        coded[here, :] = encode(piece)
+
+    for copy in row_copies + fac_copies:
         copy.wait_recv()
-    lane_r = iota((8, 128), 1)
+    lane_r = iota((16, 128), 1)
     tag_tiles = []
     for j in range((NR + 3) // 4):
-        tile = jnp.zeros((8, 128), F32)
+        tile = jnp.zeros((16, 128), F32)
         for k in range(4 * j, min(4 * j + 4, NR)):
-            tile = jnp.where(lane_r // TOKENS == k % 4, tags[k], tile)
+            tile = jnp.where(lane_r // TOKENS == k % 4, rows[k, 4 * TOKENS : 4 * TOKENS + 16, :].astype(F32), tile)
         tag_tiles.append(tile)
     tag_all = jnp.concatenate(tag_tiles, axis=1)[0:1, :MET]
     fac_tag = facs[:, :, WIDTH : WIDTH + 128].reshape(NF * BLOCK, 128)[:, 0:1].astype(F32)
     same = fac_tag == tag_all
-    met = dot(
-        facs[:, :, 0:WIDTH].reshape(NF * BLOCK, WIDTH), rows[...].reshape(MET, WIDTH), NT
+    features = jnp.concatenate(
+        [rows[:, TOKENS * j : TOKENS * j + TOKENS, :].reshape(MET, 128) for j in range(4)], axis=1
     )
+    met = dot(facs[:, :, 0:WIDTH].reshape(NF * BLOCK, WIDTH), features, NT)
     rank_part = jnp.sum(jnp.where(same, met, 0.0).reshape(NF * CAP, RANK, MET), axis=0)
     mps[...] = rank_part.astype(BF16)
     mp_copies = [
         send(mps, mprecv.at[k], mp_s.at[k], mp_r.at[k], along_mp(o)) for k, o in enumerate(MP_OFFS)
     ]
+
+    score_copies = []
+    for c in range(4):
+        here = pl.ds(64 * c, 64)
+        score_copies.append(send(coded.at[here], other.at[here], sc_s.at[c], sc_r.at[c], partner))
 
     for copy in z_copies:
         copy.wait_recv()
@@ -228,7 +246,25 @@
     second = jnp.where(upper, own_query, other_query)
     qfull[...] = (first + pltpu.roll(second, HALF, 1)).astype(BF16)
 
-    scale = 1.0 / math.sqrt(2 * HALF)
+    for copy in mp_copies:
+        copy.wait_recv()
+    rank = rank_part
+    for k in range(15):
+        rank = rank + mprecv[k].astype(F32)
+    spread = jnp.broadcast_to(rank[None], (NF * CAP, RANK, MET)).reshape(NF * BLOCK, MET)
+    spread = jnp.where(same, spread, 0.0)
+    up_all = facs[:, :, WIDTH : WIDTH + 128].reshape(NF * BLOCK, 128)
+    coarse = spread.astype(BF16)
+    rest = (spread - coarse.astype(F32)).astype(BF16)
+    delta = (dot(coarse, up_all, TN) + dot(rest, up_all, TN)).reshape(NR, TOKENS, 128)
+    low_m = iota((NR * 16, 128), 1) < HALF
+    rets[...] = jnp.where(
+        low_m, pltpu.roll(delta[:, 16:32].reshape(NR * 16, 128), HALF, 1), delta[:, 0:16].reshape(NR * 16, 128)
+    ).reshape(NR, 16, 128)
+    ret_copies = [
+        send(rets.at[k], retrecv.at[k], ret_s.at[k], ret_r.at[k], along_dp(ROW_OFFS[k], -1))
+        for k in range(1, NR)
+    ]
     len_wide = jnp.pad(len_v[...].astype(F32), ((0, 0), (0, 128 - ROWS)))
     len_col = jnp.sum(
         jnp.where(iota((QROWS, 128), 1) == iota((QROWS, 128), 0) // 16, len_wide, 0.0), axis=1, keepdims=True
@@ -237,7 +273,7 @@
     for c in range(4):
         score_copies[c].wait_recv()
         here = pl.ds(64 * c, 64)
-        scores = (own[here, :] + other[here, :]) * scale
+        scores = own[here, :] + decode(other[here, :])
         valid = iota((64, SLOTS), 1).astype(F32) < len_col[64 * c : 64 * c + 64]
         scores = jnp.where(valid, scores, MASKED_SCORE)
         top = jnp.max(scores, axis=1, keepdims=True)
@@ -277,26 +313,12 @@
     value_base = total[0:TOKENS, 128:256]
     value_base = jnp.where(upper, value_base, pltpu.roll(value_base, HALF, 1))
 
-    for copy in mp_copies:
-        copy.wait_recv()
-    rank = rank_part
-    for k in range(15):
-        rank = rank + mprecv[k].astype(F32)
-    spread = jnp.broadcast_to(rank[None], (NF * CAP, RANK, MET)).reshape(NF * BLOCK, MET)
-    spread = jnp.where(same, spread, 0.0)
-    up_all = facs[:, :, WIDTH : WIDTH + 128].reshape(NF * BLOCK, 128)
-    coarse = spread.astype(BF16)
-    rest = (spread - coarse.astype(F32)).astype(BF16)
-    rets[...] = (dot(coarse, up_all, TN) + dot(rest, up_all, TN)).reshape(NR, TOKENS, 128)
-    ret_copies = [
-        send(rets.at[k], retrecv.at[k], ret_s.at[k], ret_r.at[k], along_dp(ROW_OFFS[k], -1))
-        for k in range(1, NR)
-    ]
     lora = rets[0]
     for copy in ret_copies:
         copy.wait_recv()
     for k in range(1, NR):
         lora = lora + retrecv[k]
+    lora = jnp.concatenate([lora, pltpu.roll(lora, HALF, 1)], axis=0)
 
     new_value = ((value_base + 2.0 * lora) * norm).astype(BF16)
     new_ref[...] = jnp.where(low, key_own, ((value_base + 2.0 * lora) * norm)).astype(BF16)
@@ -307,7 +329,7 @@
         ctx_ref[:, j * 128 : j * 128 + 128] = jnp.where(low, pltpu.roll(left, HALF, 1), right).astype(BF16)
 
     for copy in (
-        row_copies + tag_copies + fac_copies + z_copies + score_copies + mp_copies + ret_copies + [q_copy, x_copy]
+        row_copies + fac_copies + z_copies + score_copies + mp_copies + ret_copies + [q_copy, x_copy]
     ):
         copy.wait_send()
 
@@ -327,8 +349,7 @@
         ((QROWS, 128), F32),
         ((QROWS, 128), BF16),
         ((QROWS, 128), BF16),
-        ((NR, TOKENS, WIDTH), BF16),
-        ((NR, 8, 128), F32),
+        ((NR, 4 * TOKENS + 16, 128), BF16),
         ((NF, BLOCK, WIDTH + 128), BF16),
         ((Z, TOKENS + 8, 256), F32),
         ((Z, TOKENS + 8, 256), F32),
@@ -336,14 +357,15 @@
         ((TOKENS + 8, 256), F32),
         ((ROWS, STEPS, WIDTH), BF16),
         ((QROWS, SLOTS), F32),
-        ((QROWS, SLOTS), F32),
+        ((QROWS, SLOTS), BF16),
+        ((QROWS, SLOTS), BF16),
         ((QROWS, 128), F32),
         ((RANK, MET), BF16),
         ((15, RANK, MET), BF16),
-        ((NR, TOKENS, 128), F32),
-        ((NR, TOKENS, 128), F32),
-    ]
-    sems = [12, NR, NR, NR, NR, NF, NF, Z, Z, 1, 1, 1, 1, 4, 4, 15, 15, NR, NR]
+        ((NR, 16, 128), F32),
+        ((NR, 16, 128), F32),
+    ]
+    sems = [12, NR, NR, NF, NF, Z, Z, 1, 1, 1, 1, 4, 4, 15, 15, NR, NR]
     any_spec = pl.BlockSpec(memory_space=pl.ANY)
     vmem_spec = pl.BlockSpec(memory_space=pltpu.VMEM)
     context, newest = pl.pallas_call(

time: 40.7 us -> 37.8 us (0.929)
  the two profiles are of different devices: /device:TPU:4 before, /device:TPU:2 now
where the time goes in v2:
time: 37.8 us; the launch traced here: 37.7 us
  Pallas kernels  35.8 us (95%)
  local copies, waits for them, and re-layouts  1.23 us (3%)
  between operations  0.64 us (2%)
    pallas_call x1, Pallas kernels, shards(): pl.pallas_call(body, out_shape=(jax.ShapeDtypeStruct((TOKENS, WIDTH), BF1...  35.8 us

profile of v2, /device:TPU:2, one launch (start us, length us, event | category | flops | bytes accessed | tf_op | source)
XLA Modules:
  0.0 37.7 jit_solution(9758440794569814995)
XLA Ops:
  0.6 35.8 %shard_map.131 = (bf16[32,512]{1,0:T(8,128)(2,1)S(1)}, bf16[32,128]{1,0:T(8,128)(2,1)S(1)}) custom-call(bf16[16,2,512]{2,1,0:T(2,128)(2,1)} %x_hbm.1, bf16[512]{0:T(512)(128)(2,1)} %gain_hbm.1, bf16[512,1024]{1,0:T(8,128)(2,1)} %k_hbm.1, bf16[512,1024]{1,0:T(8,128)(2,1)} %v_hbm.1, bf16[64,16,512]{2,1,0:T(8,128)(2,1)} %down_hbm.1, ...), custom_call_target="tpu_custom_call" | custom-call | tf_op jit(solution)/shard_map/pallas_call | solution.py:371
  36.4 0.6 %reshape.34 = bf16[16,2,1,512]{3,1,0,2:T(2,128)(2,1)} reshape(bf16[32,512]{1,0:T(8,128)(2,1)S(1)} %get-tuple-element.4) | data formatting | bytes 65536 | tf_op jit(solution)/shard_map/reshape | solution.py:397
  37.1 0.6 %copy.17 = bf16[16,2,1,128]{3,1,2,0:T(2,128)(2,1)} copy(bf16[16,2,1,128]{3,1,2,0:T(2,128)(2,1)S(1)} %bitcast.10) | data formatting | bytes 16384

commit v3 on v2

--- a/solution.py
+++ b/solution.py
@@ -321,17 +321,30 @@
     lora = jnp.concatenate([lora, pltpu.roll(lora, HALF, 1)], axis=0)
 
     new_value = ((value_base + 2.0 * lora) * norm).astype(BF16)
-    new_ref[...] = jnp.where(low, key_own, ((value_base + 2.0 * lora) * norm)).astype(BF16)
+    flat[:, 0:128] = jnp.where(low, key_own, (value_base + 2.0 * lora) * norm)
+    for r in range(ROWS):
+        new_ref[r] = flat[pl.ds(2 * r, 2), 0:128].astype(BF16)
     qexp[...] = ctxs[...] + dot(fresh_weights, new_value, NN)
     for j in range(4):
         left = qexp[pl.ds(2 * j, TOKENS, stride=GROUPS), :]
         right = qexp[pl.ds(2 * j + 1, TOKENS, stride=GROUPS), :]
-        ctx_ref[:, j * 128 : j * 128 + 128] = jnp.where(low, pltpu.roll(left, HALF, 1), right).astype(BF16)
+        flat[:, j * 128 : j * 128 + 128] = jnp.where(low, pltpu.roll(left, HALF, 1), right)
+    for r in range(ROWS):
+        ctx_ref[r] = flat[pl.ds(2 * r, 2), :].astype(BF16)
 
     for copy in (
         row_copies + fac_copies + z_copies + score_copies + mp_copies + ret_copies + [q_copy, x_copy]
     ):
         copy.wait_send()
+
+
+def place(ctx_ref, new_ref, ctx_out, new_out, sem):
+    first = pltpu.make_async_copy(ctx_ref, ctx_out, sem.at[0])
+    second = pltpu.make_async_copy(new_ref, new_out, sem.at[1])
+    first.start()
+    second.start()
+    first.wait()
+    second.wait()
 
 
 def shards(
@@ -371,8 +384,8 @@
     context, newest = pl.pallas_call(
         body,
         out_shape=(
-            jax.ShapeDtypeStruct((TOKENS, WIDTH), BF16),
-            jax.ShapeDtypeStruct((TOKENS, 128), BF16),
+            jax.ShapeDtypeStruct((ROWS, STEPS, WIDTH), BF16),
+            jax.ShapeDtypeStruct((ROWS, STEPS, 128), BF16),
         ),
         in_specs=[any_spec] * 12,
         out_specs=(vmem_spec, vmem_spec),
@@ -394,6 +407,16 @@
         queries.reshape(ROWS, STEPS, WIDTH),
         key_value_cache.reshape(ROWS, SLOTS, 128),
     )))
+    context, newest = pl.pallas_call(
+        place,
+        out_shape=(
+            pltpu.HBM((ROWS, STEPS, WIDTH), BF16),
+            pltpu.HBM((ROWS, STEPS, 128), BF16),
+        ),
+        in_specs=[any_spec, any_spec],
+        out_specs=(any_spec, any_spec),
+        scratch_shapes=[dma((2,))],
+    )(pltpu.with_memory_space_constraint(context, pltpu.VMEM), pltpu.with_memory_space_constraint(newest, pltpu.VMEM))
     return context.reshape(ROWS, STEPS, 1, WIDTH), newest.reshape(ROWS, STEPS, 1, 128)
 
 

time: 37.8 us -> 37.2 us (0.984)
  local copies, waits for them, and re-layouts: 1.23 us -> 0 us
  Pallas kernels: 35.8 us -> 36.4 us
    pallas_call x1 -> x2, Pallas kernels: 35.8 us -> 36.4 us  [the longest x1 35.8 us: shards(): pl.pallas_call(body, out_shape=(jax.ShapeDtypeStruct((ROWS, STEPS, WIDTH)...]
    reshape x1 -> x0, local copies, waits for them, and re-layouts: 0.63 us -> none  [shards(): context.reshape(ROWS, STEPS, 1, WIDTH)]
    unnamed x1 -> x0, local copies, waits for them, and re-layouts: 0.6 us -> none
where the time goes in v3:
time: 37.2 us; the launch traced here: 37.1 us
  Pallas kernels  36.4 us (98%)
  between operations  0.64 us (2%)
    pallas_call x1, Pallas kernels, shards(): pl.pallas_call(body, out_shape=(jax.ShapeDtypeStruct((ROWS, STEPS, WIDTH)...  35.8 us

profile of v3, /device:TPU:2, one launch (start us, length us, event | category | flops | bytes accessed | tf_op | source)
XLA Modules:
  0.0 37.1 jit_solution(4440756433922363304)
XLA Ops:
  0.6 35.8 %shard_map.131 = (bf16[16,2,512]{2,1,0:T(2,128)(2,1)S(1)}, bf16[16,2,128]{2,1,0:T(2,128)(2,1)S(1)}) custom-call(bf16[16,2,512]{2,1,0:T(2,128)(2,1)} %x_hbm.1, bf16[512]{0:T(512)(128)(2,1)} %gain_hbm.1, bf16[512,1024]{1,0:T(8,128)(2,1)} %k_hbm.1, bf16[512,1024]{1,0:T(8,128)(2,1)} %v_hbm.1, bf16[64,16,512]{2,1,0:T(8,128)(2,1)} %down_hbm.1, ...), custom_call_target="tpu_custom_call" | custom-call | tf_op jit(solution)/shard_map/pallas_call | solution.py:384
  36.4 0.6 %shard_map.132 = (bf16[16,2,512]{2,1,0:T(2,128)(2,1)}, bf16[16,2,128]{2,1,0:T(2,128)(2,1)}) custom-call(bf16[16,2,512]{2,1,0:T(2,128)(2,1)S(1)} %get-tuple-element.6.ctx_ref, bf16[16,2,128]{2,1,0:T(2,128)(2,1)S(1)} %get-tuple-element.7.new_ref), custom_call_target="tpu_custom_call" | custom-call | tf_op jit(solution)/shard_map/pallas_call | solution.py:410

commit v4 on v3

--- a/solution.py
+++ b/solution.py
@@ -204,6 +204,11 @@
         own[here, :] = piece
         coded[here, :] = encode(piece)
 
+    score_copies = []
+    for c in range(0, 2):
+        here = pl.ds(64 * c, 64)
+        score_copies.append(send(coded.at[here], other.at[here], sc_s.at[c], sc_r.at[c], partner))
+
     for copy in row_copies + fac_copies:
         copy.wait_recv()
     lane_r = iota((16, 128), 1)
@@ -226,8 +231,7 @@
         send(mps, mprecv.at[k], mp_s.at[k], mp_r.at[k], along_mp(o)) for k, o in enumerate(MP_OFFS)
     ]
 
-    score_copies = []
-    for c in range(4):
+    for c in range(2, 4):
         here = pl.ds(64 * c, 64)
         score_copies.append(send(coded.at[here], other.at[here], sc_s.at[c], sc_r.at[c], partner))
 
@@ -260,7 +264,7 @@
     low_m = iota((NR * 16, 128), 1) < HALF
     rets[...] = jnp.where(
         low_m, pltpu.roll(delta[:, 16:32].reshape(NR * 16, 128), HALF, 1), delta[:, 0:16].reshape(NR * 16, 128)
-    ).reshape(NR, 16, 128)
+    ).reshape(NR, 16, 128).astype(BF16)
     ret_copies = [
         send(rets.at[k], retrecv.at[k], ret_s.at[k], ret_r.at[k], along_dp(ROW_OFFS[k], -1))
         for k in range(1, NR)
@@ -313,11 +317,11 @@
     value_base = total[0:TOKENS, 128:256]
     value_base = jnp.where(upper, value_base, pltpu.roll(value_base, HALF, 1))
 
-    lora = rets[0]
+    lora = rets[0].astype(F32)
     for copy in ret_copies:
         copy.wait_recv()
     for k in range(1, NR):
-        lora = lora + retrecv[k]
+        lora = lora + retrecv[k].astype(F32)
     lora = jnp.concatenate([lora, pltpu.roll(lora, HALF, 1)], axis=0)
 
     new_value = ((value_base + 2.0 * lora) * norm).astype(BF16)
@@ -375,8 +379,8 @@
         ((QROWS, 128), F32),
         ((RANK, MET), BF16),
         ((15, RANK, MET), BF16),
-        ((NR, 16, 128), F32),
-        ((NR, 16, 128), F32),
+        ((NR, 16, 128), BF16),
+        ((NR, 16, 128), BF16),
     ]
     sems = [12, NR, NR, NF, NF, Z, Z, 1, 1, 1, 1, 4, 4, 15, 15, NR, NR]
     any_spec = pl.BlockSpec(memory_space=pl.ANY)

time: 37.2 us -> 37.1 us (level)
  no operation moved by 1% of the time
where the time goes in v4:
time: 37.1 us; the launch traced here: 37 us
  Pallas kernels  36.4 us (98%)
  between operations  0.64 us (2%)
    pallas_call x1, Pallas kernels, shards(): pl.pallas_call(body, out_shape=(jax.ShapeDtypeStruct((ROWS, STEPS, WIDTH)...  35.7 us

profile of v4, /device:TPU:2, one launch (start us, length us, event | category | flops | bytes accessed | tf_op | source)
XLA Modules:
  0.0 37.0 jit_solution(13208395635679250737)
XLA Ops:
  0.6 35.7 %shard_map.131 = (bf16[16,2,512]{2,1,0:T(2,128)(2,1)S(1)}, bf16[16,2,128]{2,1,0:T(2,128)(2,1)S(1)}) custom-call(bf16[16,2,512]{2,1,0:T(2,128)(2,1)} %x_hbm.1, bf16[512]{0:T(512)(128)(2,1)} %gain_hbm.1, bf16[512,1024]{1,0:T(8,128)(2,1)} %k_hbm.1, bf16[512,1024]{1,0:T(8,128)(2,1)} %v_hbm.1, bf16[64,16,512]{2,1,0:T(8,128)(2,1)} %down_hbm.1, ...), custom_call_target="tpu_custom_call" | custom-call | tf_op jit(solution)/shard_map/pallas_call | solution.py:388
  36.4 0.6 %shard_map.132 = (bf16[16,2,512]{2,1,0:T(2,128)(2,1)}, bf16[16,2,128]{2,1,0:T(2,128)(2,1)}) custom-call(bf16[16,2,512]{2,1,0:T(2,128)(2,1)S(1)} %get-tuple-element.6.ctx_ref, bf16[16,2,128]{2,1,0:T(2,128)(2,1)S(1)} %get-tuple-element.7.new_ref), custom_call_target="tpu_custom_call" | custom-call | tf_op jit(solution)/shard_map/pallas_call | solution.py:414

commit v5 on v4

--- a/solution.py
+++ b/solution.py
@@ -111,7 +111,7 @@
 
     for r in range(ROWS):
         flat[pl.ds(2 * r, 2), :] = x_v[r].astype(F32)
-    hidden = flat[...]
+    hidden = flat[0:TOKENS, :]
     gained = (hidden * gain_v[...].astype(F32).reshape(1, WIDTH)).astype(BF16)
     for j in range(4):
         rows[0, TOKENS * j : TOKENS * j + TOKENS, :] = gained[:, 128 * j : 128 * j + 128]
@@ -188,11 +188,11 @@
         for r in range(ROWS):
             flat[pl.ds(2 * r, 2), :] = ref[r].astype(F32)
         for g in range(GROUPS):
-            tile = flat[:, (g // 2) * 128 : (g // 2) * 128 + 128]
+            tile = flat[0:TOKENS, (g // 2) * 128 : (g // 2) * 128 + 128]
             if g % 2:
                 tile = pltpu.roll(tile, HALF, 1)
             qexp[pl.ds(g, TOKENS, stride=GROUPS), :] = jnp.where(low, tile, 0.0)
-        return qexp[...]
+        return qexp[0:QROWS, :]
 
     scale = 1.0 / math.sqrt(2 * HALF)
     own_query = expand(q_v)
@@ -325,14 +325,14 @@
     lora = jnp.concatenate([lora, pltpu.roll(lora, HALF, 1)], axis=0)
 
     new_value = ((value_base + 2.0 * lora) * norm).astype(BF16)
-    flat[:, 0:128] = jnp.where(low, key_own, (value_base + 2.0 * lora) * norm)
+    flat[0:TOKENS, 0:128] = jnp.where(low, key_own, (value_base + 2.0 * lora) * norm)
     for r in range(ROWS):
         new_ref[r] = flat[pl.ds(2 * r, 2), 0:128].astype(BF16)
-    qexp[...] = ctxs[...] + dot(fresh_weights, new_value, NN)
+    qexp[0:QROWS, :] = ctxs[...] + dot(fresh_weights, new_value, NN)
     for j in range(4):
         left = qexp[pl.ds(2 * j, TOKENS, stride=GROUPS), :]
         right = qexp[pl.ds(2 * j + 1, TOKENS, stride=GROUPS), :]
-        flat[:, j * 128 : j * 128 + 128] = jnp.where(low, pltpu.roll(left, HALF, 1), right)
+        flat[0:TOKENS, j * 128 : j * 128 + 128] = jnp.where(low, pltpu.roll(left, HALF, 1), right)
     for r in range(ROWS):
         ctx_ref[r] = flat[pl.ds(2 * r, 2), :].astype(BF16)
 
@@ -362,8 +362,8 @@
         ((1, ROWS), jnp.int32), ((1, ROWS), jnp.int32), ((ROWS, STEPS, WIDTH), BF16), ((ROWS, SLOTS, 128), BF16),
     ]
     work = [
-        ((TOKENS, WIDTH), F32),
-        ((QROWS, 128), F32),
+        ((TOKENS + 8, WIDTH), F32),
+        ((QROWS + 8, 128), F32),
         ((QROWS, 128), BF16),
         ((QROWS, 128), BF16),
         ((NR, 4 * TOKENS + 16, 128), BF16),

time: 37.1 us -> 37.1 us (level)
  no operation moved by 1% of the time
where the time goes in v5:
time: 37.1 us; the launch traced here: 37 us
  Pallas kernels  36.4 us (98%)
  between operations  0.64 us (2%)
    pallas_call x1, Pallas kernels, shards(): pl.pallas_call(body, out_shape=(jax.ShapeDtypeStruct((ROWS, STEPS, WIDTH)...  35.7 us

profile of v5, /device:TPU:2, one launch (start us, length us, event | category | flops | bytes accessed | tf_op | source)
XLA Modules:
  0.0 37.0 jit_solution(8511737347696416048)
XLA Ops:
  0.6 35.7 %shard_map.131 = (bf16[16,2,512]{2,1,0:T(2,128)(2,1)S(1)}, bf16[16,2,128]{2,1,0:T(2,128)(2,1)S(1)}) custom-call(bf16[16,2,512]{2,1,0:T(2,128)(2,1)} %x_hbm.1, bf16[512]{0:T(512)(128)(2,1)} %gain_hbm.1, bf16[512,1024]{1,0:T(8,128)(2,1)} %k_hbm.1, bf16[512,1024]{1,0:T(8,128)(2,1)} %v_hbm.1, bf16[64,16,512]{2,1,0:T(8,128)(2,1)} %down_hbm.1, ...), custom_call_target="tpu_custom_call" | custom-call | tf_op jit(solution)/shard_map/pallas_call | solution.py:388
  36.4 0.6 %shard_map.132 = (bf16[16,2,512]{2,1,0:T(2,128)(2,1)}, bf16[16,2,128]{2,1,0:T(2,128)(2,1)}) custom-call(bf16[16,2,512]{2,1,0:T(2,128)(2,1)S(1)} %get-tuple-element.6.ctx_ref, bf16[16,2,128]{2,1,0:T(2,128)(2,1)S(1)} %get-tuple-element.7.new_ref), custom_call_target="tpu_custom_call" | custom-call | tf_op jit(solution)/shard_map/pallas_call | solution.py:414
